TPU v7x, 32 devices: a whole 2x2x4 slice. The times are simulated.
32 devices in a mesh: pair: 2 (over core), virt: 16 (over z, y, x).
Axes of the slice: x: 2, y: 2, z: 4, core: 2. Of those that a mesh axis runs over, the one named last changes fastest.
Arguments:
- amplitudes: bfloat16 [512, 32768], P('virt', 'pair'), may hold values from -6 to 6
- integrals: bfloat16 [32768, 32768], P('virt', 'pair'), may hold values from -0.03125 to 0.03125
- cycle_integrals: bfloat16 [16384, 16384], P('pair', 'virt'), may hold values from -0.125 to 0.125
- virt_count: int32 [8], replicated, may hold values from 32 to 64, as said below
Outputs:
- ladder: bfloat16 [512, 32768], P(None, 'virt')
- cycle: bfloat16 [8192, 16384], P('pair', 'virt')
Inputs may be any that keep to these rules, and one draw needn't show every extreme that they name: `virt_count`: every irrep keeps at least half of its 64 slots; some irrep has all 64 and some has exactly half.
All inputs are finite; a program needn't handle non-finite values.
Results may differ from a plain program's by a relative error of at most 0.0049.
Values may be sent and summed in bfloat16 or wider, within the bound.
A program may use at most 256 MiB of HBM per device.

v0:
```python
import jax
import jax.numpy as jnp
from jax import lax
from jax.sharding import PartitionSpec as P

VH = 64
OI = 16
OJ = 32


def irrep_sizes(virt_count, irrep_of):
    irrep_ids = jnp.arange(virt_count.shape[0], dtype=jnp.int32)
    return jnp.sum(
        jnp.where(irrep_of[:, None] == irrep_ids[None, :], virt_count[None, :], 0), axis=1
    )


def pair_mask(virt_count, first_pos, length, slot_width):
    position = first_pos + jnp.arange(length, dtype=jnp.int32)
    irrep_of = position // (slot_width * slot_width)
    slot_one = position // slot_width % slot_width
    slot_two = position % slot_width
    irrep_size = irrep_sizes(virt_count, irrep_of)
    return ((slot_one < irrep_size) & (slot_two < irrep_size)).astype(jnp.float32)


def slot_mask(virt_count, first_pos, length, slot_width):
    position = (first_pos + jnp.arange(length, dtype=jnp.int32)) % (
        virt_count.shape[0] * slot_width
    )
    irrep_of = position // slot_width
    slot_ids = position % slot_width
    return (slot_ids < irrep_sizes(virt_count, irrep_of)).astype(jnp.float32)


def body(amplitudes, integrals, cycle_integrals, virt_count):
    slot_width = VH
    irrep_total = virt_count.shape[0]
    group_width = irrep_total * slot_width
    pair_devs = lax.axis_size("pair")
    ab_count = integrals.shape[0]
    cd_count = integrals.shape[1]
    jb_count = cycle_integrals.shape[1]
    cd_first = lax.axis_index("pair") * cd_count
    ab_first = lax.axis_index("virt") * ab_count
    a_count = ab_count // slot_width
    per_irrep = slot_width * slot_width // ab_count
    masked = amplitudes * pair_mask(virt_count, cd_first, cd_count, slot_width)[None, :].astype(
        jnp.bfloat16
    )
    partial_sums = lax.dot_general(
        lax.all_gather(masked, "virt", axis=0, tiled=True),
        integrals,
        (((1,), (1,)), ((), ())),
        preferred_element_type=jnp.float32,
    )
    keep_pairs = pair_mask(virt_count, ab_first, ab_count, slot_width)[None, :]
    ladder_total = lax.psum(partial_sums, "pair")
    ladder = (ladder_total * keep_pairs).astype(jnp.bfloat16)
    keep_cols = slot_mask(virt_count, lax.axis_index("virt") * jb_count, jb_count, slot_width)[
        None, :
    ]
    pair_rows = ladder.reshape(OI, OJ, ab_count)
    k_local = OJ // pair_devs
    own_k = lax.dynamic_slice_in_dim(pair_rows, lax.axis_index("pair") * k_local, k_local, 1)[None]
    cycle_local = cycle_integrals.reshape(k_local, irrep_total, slot_width, jb_count)
    shards = lax.all_gather(own_k, "virt", axis=0, tiled=True)
    shard_count = shards.shape[0]
    irrep_ids = jnp.arange(shard_count, dtype=jnp.int32) * ab_count // (slot_width * slot_width)
    chosen = jnp.take(cycle_local, irrep_ids, axis=1)
    amp_block = shards.reshape(shard_count, OI, k_local, a_count, slot_width)
    pieces = jnp.einsum("sikac,kscj->siaj", amp_block, chosen, preferred_element_type=jnp.float32)
    full_term = jnp.transpose(
        pieces.reshape(irrep_total, per_irrep, OI, a_count, jb_count), (2, 0, 1, 3, 4)
    )
    full_term = full_term.reshape(OI * group_width, jb_count)
    summed = lax.psum_scatter(full_term, "pair", scatter_dimension=0, tiled=True)
    cycle = (summed * keep_cols).astype(jnp.bfloat16)
    return (ladder, cycle)


def solution(mesh):
    placed = (P("virt", "pair"), P("virt", "pair"), P("pair", "virt"), P())
    return jax.shard_map(
        body,
        mesh=mesh,
        in_specs=placed,
        out_specs=(P(None, "virt"), P("pair", "virt")),
        check_vma=False,
    )
```

profile of v0, /device:TPU:1, one launch (start us, length us, event | category | flops | bytes accessed | tf_op | source)
XLA Modules:
  0.0 645.9 jit_solution(7602684747617650595)
XLA Ops:
  7.2 0.0 all-gather.4.cloned.1.call-start
  7.3 0.9 select_reduce_fusion
  8.2 0.1 convert_convert_fusion
  8.3 2.3 broadcast_multiply_fusion
  10.6 0.0 all-gather.4.cloned.1.call-update
  10.6 0.0 copy-start.1
  10.6 0.0 all-reduce.2.cloned.1.call-start
  10.7 194.0 %all-gather.4.cloned.1.call-done = bf16[512,16384]{1,0:T(8,128)(2,1)} async-done(((bf16[32,16384]{1,0:T(8,128)(2,1)}), bf16[512,16384]{1,0:T(8,128)(2,1)}) %all-gather.4.cloned.1.call-update) | async-done | bytes 16777232 | tf_op jit(solution)/shard_map/all_gather | solution.py:52
  204.7 44.1 %fusion.40 = f32[512,2048]{1,0:T(8,128)} fusion(bf16[512,16384]{1,0:T(8,128)(2,1)} %all-gather.4.cloned.1.call-done, bf16[2048,16384]{1,0:T(8,128)(2,1)} %param.5), kind=kOutput, calls=%fused_computation.100 | convolution fusion | flops 34359738368 | bytes 88080384 | tf_op jit(solution)/shard_map/dot_general | solution.py:51
  248.8 0.0 all-reduce.2.cloned.1.call-update
  248.8 0.0 all-gather.6.cloned.1.call-start
  248.9 0.0 copy-done.1
  248.9 0.1 select_reduce_fusion.1
  249.0 27.4 %all-reduce.2.cloned.1.call-done = f32[512,2048]{1,0:T(8,128)} async-done(((f32[512,2048]{1,0:T(8,128)}), f32[512,2048]{1,0:T(8,128)}) %all-reduce.2.cloned.1.call-update) | async-done | bytes 4194320 | tf_op jit(solution)/shard_map/psum | solution.py:58
  276.4 2.7 multiply_convert_fusion.1
  279.0 0.0 copy-start
  279.0 1.1 constant_dynamic-slice_fusion
  280.2 0.0 all-gather.6.cloned.1.call-update
  280.2 0.2 reduce-scatter.2.cloned.1.call-start
  280.5 12.0 %fusion.39 = (bf16[16,8,64,512]{3,2,1,0:T(8,128)(2,1)}, bf16[16,8,64,512]{3,2,1,0:T(8,128)(2,1)}) fusion(bf16[16,8,64,1024]{3,2,1,0:T(8,128)(2,1)} %bitcast.26), kind=kLoop, calls=%fused_computation.99 | loop fusion | bytes 33554432 | tf_op jit(solution)/shard_map/jit(_take)/gather | solution.py:70
  292.5 0.0 copy-done
  292.5 10.7 %gather_fusion = bf16[16,16,64,512]{3,2,1,0:T(8,128)(2,1)} fusion(bf16[16,8,64,512]{3,2,1,0:T(8,128)(2,1)} %get-tuple-element.2, s32[1024]{0:T(1024)S(1)} %pad_clamp_fusion), kind=kCustom, calls=%fused_computation | custom fusion | bytes 33554496 | tf_op jit(solution)/shard_map/jit(_take)/gather | solution.py:70
  303.2 10.8 %gather_fusion.1 = bf16[16,16,64,512]{3,2,1,0:T(8,128)(2,1)} fusion(bf16[16,8,64,512]{3,2,1,0:T(8,128)(2,1)} %get-tuple-element.3, s32[1024]{0:T(1024)S(1)} %pad_clamp_fusion), kind=kCustom, calls=%fused_computation.1 | custom fusion | bytes 33554496 | tf_op jit(solution)/shard_map/jit(_take)/gather | solution.py:70
  314.0 158.4 %all-gather.6.cloned.1.call-done = bf16[256,16,2048]{2,1,0:T(8,128)(2,1)} async-done(((bf16[16,16,2048]{2,1,0:T(8,128)(2,1)}), bf16[256,16,2048]{2,1,0:T(8,128)(2,1)}) %all-gather.6.cloned.1.call-update) | async-done | bytes 16777232 | tf_op jit(solution)/shard_map/all_gather | solution.py:67
  472.4 47.7 %reshape.281 = bf16[16,16,16,32,64]{4,3,2,1,0:T(8,128)(2,1)} reshape(bf16[256,16,2048]{2,1,0:T(8,128)(2,1)} %all-gather.6.cloned.1.call-done) | data formatting | bytes 33554432 | tf_op jit(solution)/shard_map/reshape | solution.py:71
  520.1 42.5 %fusion.1 = f32[16,16,32,1024,1]{3,2,4,1,0:T(8,128)} fusion(bf16[16,16,16,32,64]{4,3,2,1,0:T(8,128)(2,1)} %reshape.281, bf16[16,16,64,512]{3,2,0,1:T(8,128)(2,1)} %bitcast.28, bf16[16,16,64,512]{3,2,0,1:T(8,128)(2,1)} %bitcast.27, pred[16]{0:T(512)(128)(4,1)S(1)} %compare_and_fusion), kind=kOutput, calls=%fused_computation.4 | convolution fusion | flops 17263755264 | bytes 83886096 | tf_op jit(solution)/shard_map/sikac,kscj->siaj/dot_general | solution.py:72
  562.6 23.3 %copy.8 = f32[16,8,2,32,1024]{4,3,2,1,0:T(8,128)} copy(f32[16,8,2,32,1024]{4,3,0,2,1:T(8,128)} %bitcast.25) | data formatting | bytes 67108864 | tf_op jit(solution)/shard_map/transpose | solution.py:73
  585.9 0.0 reduce-scatter.2.cloned.1.call-update
  585.9 0.1 select_reduce_fusion.2
  586.1 44.2 %reduce-scatter.2.cloned.1.call-done = f32[4096,1024]{1,0:T(8,128)} async-done(((f32[8192,1024]{1,0:T(8,128)}), f32[4096,1024]{1,0:T(8,128)}) %reduce-scatter.2.cloned.1.call-update) | async-done | bytes 16777232 | tf_op jit(solution)/shard_map/reduce_scatter | solution.py:77
  630.3 9.1 %multiply_convert_fusion = bf16[4096,1024]{1,0:T(8,128)(2,1)} fusion(f32[4096,1024]{1,0:T(8,128)} %reduce-scatter.2.cloned.1.call-done, f32[1024]{0:T(1024)S(1)} %fusion.34), kind=kLoop, calls=%fused_computation.8 | loop fusion | flops 8388608 | bytes 25169920 | tf_op jit(solution)/shard_map/convert_element_type | solution.py:78
  (8 shorter events, 0.1 us)
Async XLA Ops:
  7.2 197.5 %all-gather.4.cloned.1.call-start = ((), (), s32[]{:S(2)}) async-start(), calls=%async_computation.1 | async-start | bytes 17825792 | tf_op jit(solution)/shard_map/all_gather | solution.py:52
  10.6 238.2 %copy-start.1 = (s32[8]{0:T(128)S(1)}, s32[8]{0:T(128)}, u32[]{:S(2)}) copy-start(s32[8]{0:T(128)} %param.7) | copy-start | bytes 100
  10.6 265.7 %all-reduce.2.cloned.1.call-start = ((), (), s32[]{:S(2)}) async-start(), calls=%async_computation.2 | async-start | bytes 8388608 | tf_op jit(solution)/shard_map/psum | solution.py:58
  248.8 223.6 %all-gather.6.cloned.1.call-start = ((), (), s32[]{:S(2)}) async-start(), calls=%async_computation.4 | async-start | bytes 17825792 | tf_op jit(solution)/shard_map/all_gather | solution.py:67
  279.0 13.5 %copy-start = (bf16[512,2048]{1,0:T(8,128)(2,1)}, bf16[512,2048]{1,0:T(8,128)(2,1)S(1)}, u32[]{:S(2)}) copy-start(bf16[512,2048]{1,0:T(8,128)(2,1)S(1)} %multiply_convert_fusion.1) | copy-start | bytes 6291460
  280.2 350.0 %reduce-scatter.2.cloned.1.call-start = ((), (), s32[]{:S(2)}) async-start(), calls=%async_computation.3 | async-start | bytes 50331648 | tf_op jit(solution)/shard_map/reduce_scatter | solution.py:77
Sparse Core Ops, SparseCore 0:
  11.3 193.2 all-gather.3
  248.9 27.3 all-reduce.1
  280.3 191.9 all-gather.5
  586.0 44.1 reduce-scatter.1
where the time goes:
time: 648 us; the launch traced here: 646 us
  waiting for transfers between devices  424 us (65%)
  local copies, waits for them, and re-layouts  106 us (16%)
  matrix products  86.6 us (13%)
  other arithmetic  15.4 us (2%)
  between operations  13.9 us (2%)
    all_gather x1, waiting for transfers between devices, body(): lax.all_gather(masked, 'virt', axis=0, tiled=True)  194 us
    all_gather x1, waiting for transfers between devices, body(): shards = lax.all_gather(own_k, 'virt', axis=0, tiled=True)  158 us
    reshape x1, local copies, waits for them, and re-layouts, body(): amp_block = shards.reshape(shard_count, OI, k_local, a_count, slot_width)  47.7 us
    reduce_scatter x1, waiting for transfers between devices, body(): lax.psum_scatter(full_term, 'pair', scatter_dimension=0, tiled=True)  44.2 us
    dot_general x1, matrix products, body(): lax.dot_general(lax.all_gather(masked, 'virt', axis=0, tiled=True), integ...  44.1 us
    dot_general x1, matrix products, body(): jnp.einsum('sikac,kscj->siaj', amp_block, chosen, preferred_element_type=...  42.5 us
    gather x3, local copies, waits for them, and re-layouts, body(): chosen = jnp.take(cycle_local, irrep_ids, axis=1)  33.5 us
    psum x1, waiting for transfers between devices, body(): ladder_total = lax.psum(partial_sums, 'pair')  27.4 us
  transfers between devices with their start and end apart: 4, of which 4 were waited for; matrix products, arithmetic and copies ran while one was open for 5% of the time, Pallas kernels for 0%

commit v1 on v0

v1 whole, which is shorter than its diff:
```python
import functools

import jax
import jax.numpy as jnp
from jax import lax
from jax.experimental import pallas as pl
from jax.experimental.pallas import tpu as pltpu
from jax.sharding import PartitionSpec as P

VH = 64
OI = 16
OJ = 32
MESH = pl.DeviceIdType.MESH
CHUNK = 1024
PARTS = ((0, 384), (384, 384), (768, 256))


def irrep_sizes(virt_count, irrep_of):
    irrep_ids = jnp.arange(virt_count.shape[0], dtype=jnp.int32)
    return jnp.sum(
        jnp.where(irrep_of[:, None] == irrep_ids[None, :], virt_count[None, :], 0), axis=1
    )


def pair_mask(virt_count, first_pos, length, slot_width):
    position = first_pos + jnp.arange(length, dtype=jnp.int32)
    irrep_of = position // (slot_width * slot_width)
    slot_one = position // slot_width % slot_width
    slot_two = position % slot_width
    irrep_size = irrep_sizes(virt_count, irrep_of)
    return ((slot_one < irrep_size) & (slot_two < irrep_size)).astype(jnp.float32)


def slot_mask(virt_count, first_pos, length, slot_width):
    position = (first_pos + jnp.arange(length, dtype=jnp.int32)) % (
        virt_count.shape[0] * slot_width
    )
    irrep_of = position // slot_width
    slot_ids = position % slot_width
    return (slot_ids < irrep_sizes(virt_count, irrep_of)).astype(jnp.float32)


def bit_reverse(value, bits):
    out = value * 0
    for b in range(bits):
        out = out + ((value >> b) & 1) * (1 << (bits - 1 - b))
    return out


def place_of(device, bits):
    return (device >> 1) & 1, device & 1, bit_reverse(device >> 2, bits - 2)


def bit_orders(bits):
    high = list(range(bits - 1, 1, -1))
    return (high + [0, 1], high + [1, 0], [0, 1] + high)


def merge_rows(x):
    rows = 1
    for s in x.shape[:-1]:
        rows *= s
    if x.shape[-2] % 16:
        return x.astype(jnp.float32).reshape(rows, x.shape[-1]).astype(x.dtype)
    return x.reshape(rows, x.shape[-1])


def barrier(bits, me, pair):
    sem = pltpu.get_barrier_semaphore()
    for b in range(bits):
        pl.semaphore_signal(
            sem, inc=1, device_id={"virt": me ^ (1 << b), "pair": pair}, device_id_type=MESH
        )
    pl.semaphore_signal(
        sem, inc=1, device_id={"virt": me, "pair": 1 - pair}, device_id_type=MESH
    )
    pl.semaphore_wait(sem, bits + 1)


def gather_copy(buf_at, bits, me, pair, send_sem, recv_sem, chunk, part, step):
    order = bit_orders(bits)[part]
    done = order[:step]
    y, x, r = place_of(me, bits)
    high = len([b for b in done if b > 1])
    off, width = PARTS[part]
    at_y = pl.ds(0, 2) if 1 in done else pl.ds(y, 1)
    at_x = pl.ds(0, 2) if 0 in done else pl.ds(x, 1)
    at_r = pl.ds((r >> high) << high, 1 << high)
    region = buf_at(chunk, at_y, at_x, at_r, pl.ds(off, width))
    return pltpu.make_async_remote_copy(
        src_ref=region,
        dst_ref=region,
        send_sem=send_sem.at[chunk, part, step],
        recv_sem=recv_sem.at[chunk, part, step],
        device_id={"virt": me ^ (1 << order[step]), "pair": pair},
        device_id_type=MESH,
    )


def gather_waves(chunks, bits, copy_of, own_ready, use):
    parts = range(len(PARTS))
    lag = 2
    for tick in range(chunks + lag * bits):
        for step in range(bits, -1, -1):
            chunk = tick - lag * step
            if not 0 <= chunk < chunks:
                continue
            if step == 0:
                own_ready(chunk)
            else:
                for part in parts:
                    copy_of(chunk, part, step - 1).wait_recv()
            if step < bits:
                for part in parts:
                    copy_of(chunk, part, step).start()
        chunk = tick - lag * bits
        if 0 <= chunk < chunks:
            use(chunk)
    for chunk in range(chunks):
        for part in parts:
            for step in range(bits):
                copy_of(chunk, part, step).wait_send()


def ladder_kernel(bits, amp_ref, w_ref, out_ref, held, w_buf, acc, away, near,
                  own_sem, w_sem, send_sem, recv_sem, sum_send, sum_recv, fin_send, fin_recv):
    me = lax.axis_index("virt")
    pair = lax.axis_index("pair")
    chunks = held.shape[0]
    slots = w_buf.shape[0]
    tiles, rows, tile = acc.shape
    half = rows // 2
    y, x, r = place_of(me, bits)

    def own_copy(c):
        return pltpu.make_async_copy(
            amp_ref.at[:, pl.ds(c * CHUNK, CHUNK)], held.at[c, y, x, r], own_sem.at[c]
        )

    def w_copy(c):
        return pltpu.make_async_copy(
            w_ref.at[:, pl.ds(c * CHUNK, CHUNK)], w_buf.at[c % slots], w_sem.at[c % slots]
        )

    def buf_at(c, at_y, at_x, at_r, cols):
        return held.at[c, at_y, at_x, at_r, :, cols]

    def copy_of(c, part, step):
        return gather_copy(buf_at, bits, me, pair, send_sem, recv_sem, c, part, step)

    for c in range(chunks):
        own_copy(c).start()
    for c in range(min(slots, chunks)):
        w_copy(c).start()
    barrier(bits, me, pair)

    def sum_copy(n):
        return pltpu.make_async_remote_copy(
            src_ref=away.at[n], dst_ref=near.at[n], send_sem=sum_send.at[n],
            recv_sem=sum_recv.at[n], device_id={"virt": me, "pair": 1 - pair},
            device_id_type=MESH,
        )

    def fin_copy(n):
        region = out_ref.at[n, pair]
        return pltpu.make_async_remote_copy(
            src_ref=region, dst_ref=region, send_sem=fin_send.at[n],
            recv_sem=fin_recv.at[n], device_id={"virt": me, "pair": 1 - pair},
            device_id_type=MESH,
        )

    def use(c):
        w_copy(c).wait()

        @pl.loop(0, tiles)
        def _(n):
            at = pl.ds(pl.multiple_of(n * tile, tile), tile)
            part = lax.dot_general(
                merge_rows(held[c]), w_buf[c % slots, at, :], (((1,), (1,)), ((), ())),
                preferred_element_type=jnp.float32,
            )
            acc[n] = part if c == 0 else acc[n] + part
            if c == chunks - 1:
                away[n] = acc[n, pl.ds(pl.multiple_of((1 - pair) * half, half), half), :]
                sum_copy(n).start()

        if c + slots < chunks:
            w_copy(c + slots).start()

    gather_waves(chunks, bits, copy_of, lambda c: own_copy(c).wait(), use)

    @pl.loop(0, tiles)
    def _(n):
        sum_copy(n).wait()
        total = acc[n, pl.ds(pl.multiple_of(pair * half, half), half), :] + near[n]
        out_ref[n, pair] = total.astype(out_ref.dtype)
        fin_copy(n).start()

    @pl.loop(0, tiles)
    def _(n):
        fin_copy(n).wait()


def cycle_kernel(bits, u_ref, m_ref, out_ref, held, m_buf, away, near, own,
                 own_sem, m_sem, out_sem, send_sem, recv_sem, sum_send, sum_recv):
    me = lax.axis_index("virt")
    pair = lax.axis_index("pair")
    chunks = held.shape[1]
    groups, irreps, rows, cols = away.shape
    per_group = chunks // groups
    a_count = held.shape[5]
    per_irrep = (1 << bits) // irreps
    tile = min(256, cols)
    y, x, r = place_of(me, bits)

    def own_copy(c):
        return pltpu.make_async_copy(u_ref.at[:, c], held.at[:, c, y, x, r], own_sem.at[c])

    def m_copy(h):
        return pltpu.make_async_copy(m_ref.at[:, h], m_buf.at[h], m_sem.at[h])

    def buf_at(c, at_y, at_x, at_r, at_cols):
        return held.at[:, c, at_y, at_x, at_r, :, at_cols]

    def copy_of(c, part, step):
        return gather_copy(buf_at, bits, me, pair, send_sem, recv_sem, c, part, step)

    for c in range(chunks):
        own_copy(c).start()
    for h in range(irreps):
        m_copy(h).start()
    barrier(bits, me, pair)

    def sum_copy(g, h):
        return pltpu.make_async_remote_copy(
            src_ref=away.at[g, h], dst_ref=near.at[g, h], send_sem=sum_send.at[g, h],
            recv_sem=sum_recv.at[g, h], device_id={"virt": me, "pair": 1 - pair},
            device_id_type=MESH,
        )

    def out_copy(g, h, j):
        size = rows // per_group
        return pltpu.make_async_copy(
            near.at[g, h, pl.ds(j * size, size), :],
            out_ref.at[g * per_group + j, h], out_sem.at[g, h, j],
        )

    def finish(g):
        @pl.loop(0, irreps)
        def _(h):
            sum_copy(g, h).wait_recv()
            near[g, h] = (own[h] + near[g, h].astype(jnp.float32)).astype(near.dtype)
            for j in range(per_group):
                out_copy(g, h, j).start()

    def use(c):
        if (c + 1) % per_group:
            return
        g = c // per_group
        if g:
            finish(g - 1)

        @pl.loop(0, irreps)
        def _(h):
            if g == 0:
                m_copy(h).wait()
            pieces = []
            for side in (1 - pair, pair):
                for j in range(per_group):
                    for s in range(per_irrep):
                        py, px, pr = place_of(h * per_irrep + s, bits)
                        pieces.append(held[side, g * per_group + j, py, px, pr])
            left = merge_rows(jnp.stack(pieces))
            for n in range(cols // tile):
                at = pl.ds(n * tile, tile)
                part = jnp.dot(
                    left, merge_rows(m_buf[h, :, :, at]), preferred_element_type=jnp.float32
                )
                away[g, h, :, at] = part[:rows].astype(away.dtype)
                own[h, :, at] = part[rows:]
            sum_copy(g, h).start()

    gather_waves(chunks, bits, copy_of, lambda c: own_copy(c).wait(), use)
    finish(groups - 1)
    for g in range(groups):
        @pl.loop(0, irreps)
        def _(h):
            sum_copy(g, h).wait_send()
            for j in range(per_group):
                out_copy(g, h, j).wait()


def body(amplitudes, integrals, cycle_integrals, virt_count):
    slot_width = VH
    irrep_total = virt_count.shape[0]
    virt_devs = lax.axis_size("virt")
    bits = virt_devs.bit_length() - 1
    pair_devs = lax.axis_size("pair")
    ab_count, cd_count = integrals.shape
    jb_count = cycle_integrals.shape[1]
    p_rows = amplitudes.shape[0]
    p_all = p_rows * virt_devs
    pair = lax.axis_index("pair")
    virt = lax.axis_index("virt")
    dma = pltpu.SemaphoreType.DMA
    any_spec = pl.BlockSpec(memory_space=pl.ANY)
    parts = len(PARTS)
    masked = amplitudes * pair_mask(virt_count, pair * cd_count, cd_count, slot_width)[
        None, :
    ].astype(jnp.bfloat16)
    chunks = cd_count // CHUNK
    tile = min(256, ab_count)
    tiles = ab_count // tile
    half = p_all // 2
    raw = pl.pallas_call(
        functools.partial(ladder_kernel, bits),
        out_shape=jax.ShapeDtypeStruct((tiles, 2, half, tile), jnp.bfloat16),
        in_specs=[any_spec, any_spec],
        out_specs=pl.BlockSpec(memory_space=pltpu.VMEM),
        scratch_shapes=[
            pltpu.VMEM((chunks, 2, 2, virt_devs // 4, p_rows, CHUNK), jnp.bfloat16),
            pltpu.VMEM((3, ab_count, CHUNK), jnp.bfloat16),
            pltpu.VMEM((tiles, p_all, tile), jnp.float32),
            pltpu.VMEM((tiles, half, tile), jnp.float32),
            pltpu.VMEM((tiles, half, tile), jnp.float32),
            dma((chunks,)),
            dma((3,)),
            dma((chunks, parts, bits)),
            dma((chunks, parts, bits)),
            dma((tiles,)),
            dma((tiles,)),
            dma((tiles,)),
            dma((tiles,)),
        ],
        compiler_params=pltpu.CompilerParams(
            collective_id=0, has_side_effects=True, vmem_limit_bytes=56 * 2**20
        ),
        cost_estimate=pl.CostEstimate(
            flops=2 * p_all * ab_count * cd_count,
            bytes_accessed=2 * ab_count * cd_count,
            transcendentals=0,
        ),
        name="ladder",
    )(masked, integrals)
    grid = raw.reshape((tiles,) + (2,) * bits + (p_rows, tile))
    order = tuple(range(bits, 2, -1)) + (1, 2, bits + 1, 0, bits + 2)
    rows = jnp.transpose(grid, order).reshape(p_all, ab_count)
    keep_pairs = pair_mask(virt_count, virt * ab_count, ab_count, slot_width)[None, :]
    ladder = rows * keep_pairs.astype(jnp.bfloat16)

    a_count = ab_count // slot_width
    k_local = OJ // pair_devs
    half_i = OI // 2
    own_k = lax.dynamic_slice_in_dim(
        ladder.reshape(2, half_i, OJ, a_count, slot_width), pair * k_local, k_local, 2
    )
    sent = jnp.transpose(own_k, (0, 1, 3, 2, 4)).reshape(
        2, half_i, a_count, k_local * slot_width
    )
    groups = half_i // 2
    out_rows = half_i // groups * slot_width
    depth = k_local * slot_width
    cycle = pl.pallas_call(
        functools.partial(cycle_kernel, bits),
        out_shape=jax.ShapeDtypeStruct(
            (half_i, irrep_total, slot_width, jb_count), jnp.bfloat16
        ),
        in_specs=[any_spec, any_spec],
        out_specs=any_spec,
        scratch_shapes=[
            pltpu.VMEM((2, half_i, 2, 2, virt_devs // 4, a_count, depth), jnp.bfloat16),
            pltpu.VMEM((irrep_total, k_local, slot_width, jb_count), jnp.bfloat16),
            pltpu.VMEM((groups, irrep_total, out_rows, jb_count), jnp.bfloat16),
            pltpu.VMEM((groups, irrep_total, out_rows, jb_count), jnp.bfloat16),
            pltpu.VMEM((irrep_total, out_rows, jb_count), jnp.float32),
            dma((half_i,)),
            dma((irrep_total,)),
            dma((groups, irrep_total, 2)),
            dma((half_i, parts, bits)),
            dma((half_i, parts, bits)),
            dma((groups, irrep_total)),
            dma((groups, irrep_total)),
        ],
        compiler_params=pltpu.CompilerParams(
            collective_id=1, has_side_effects=True, vmem_limit_bytes=58 * 2**20
        ),
        cost_estimate=pl.CostEstimate(
            flops=2 * OI * irrep_total * slot_width * depth * jb_count,
            bytes_accessed=4 * irrep_total * depth * jb_count,
            transcendentals=0,
        ),
        name="cycle",
    )(sent, cycle_integrals.reshape(k_local, irrep_total, slot_width, jb_count))
    keep_cols = slot_mask(virt_count, virt * jb_count, jb_count, slot_width)[None, :]
    cycle = cycle.reshape(half_i * irrep_total * slot_width, jb_count) * keep_cols.astype(
        jnp.bfloat16
    )
    return (ladder, cycle)


def solution(mesh):
    placed = (P("virt", "pair"), P("virt", "pair"), P("pair", "virt"), P())
    return jax.shard_map(
        body,
        mesh=mesh,
        in_specs=placed,
        out_specs=(P(None, "virt"), P("pair", "virt")),
        check_vma=False,
    )
```

time: 648 us -> 314 us (0.48)
  waiting for transfers between devices: 424 us -> 0 us
  Pallas kernels: 0 us -> 287 us
  local copies, waits for them, and re-layouts: 106 us -> 10.1 us
  matrix products: 86.6 us -> 0 us
  between operations: 13.9 us -> 0.72 us
    all_gather x2 -> x0, waiting for transfers between devices: 352 us -> none  [the longest x1 194 us: body(): lax.all_gather(masked, 'virt', axis=0, tiled=True)]
    pallas_call x0 -> x2, Pallas kernels: none -> 287 us  [the longest x1 145 us: body(): pl.pallas_call(functools.partial(cycle_kernel, bits), out_shape=jax.Shape...]
    dot_general x2 -> x0, matrix products: 86.6 us -> none  [the longest x1 44.1 us: body(): lax.dot_general(lax.all_gather(masked, 'virt', axis=0, tiled=True), integ...]
    reduce_scatter x1 -> x0, waiting for transfers between devices: 44.2 us -> none  [body(): lax.psum_scatter(full_term, 'pair', scatter_dimension=0, tiled=True)]
    reshape x1 -> x3, local copies, waits for them, and re-layouts: 47.7 us -> 8.46 us  [the longest x1 3.17 us: body(): rows = jnp.transpose(grid, order).reshape(p_all, ab_count)]
    gather x3 -> x0, local copies, waits for them, and re-layouts: 33.5 us -> none  [body(): chosen = jnp.take(cycle_local, irrep_ids, axis=1)]
    psum x1 -> x0, waiting for transfers between devices: 27.4 us -> none  [body(): ladder_total = lax.psum(partial_sums, 'pair')]
    transpose x1, local copies, waits for them, and re-layouts: 23.3 us -> 0.89 us  [body(): jnp.transpose(own_k, (0, 1, 3, 2, 4))]
  transfers between devices with their start and end apart: 4 -> 0, of which waited for: 4 -> 0; matrix products, arithmetic and copies ran while one was open for 5% -> 0% of each run, Pallas kernels for 0% -> 0%
where the time goes in v1:
time: 314 us; the launch traced here: 313 us
  Pallas kernels  287 us (91%)
  other arithmetic  15.5 us (5%)
  local copies, waits for them, and re-layouts  10.1 us (3%)
    pallas_call x1, Pallas kernels, body(): pl.pallas_call(functools.partial(cycle_kernel, bits), out_shape=jax.Shape...  145 us
    pallas_call x1, Pallas kernels, body(): pl.pallas_call(functools.partial(ladder_kernel, bits), out_shape=jax.Shap...  142 us
    mul x1, other arithmetic, body(): cycle.reshape(half_i * irrep_total * slot_width, jb_count)  7.32 us

profile of v1, /device:TPU:1, one launch (start us, length us, event | category | flops | bytes accessed | tf_op | source)
XLA Modules:
  0.0 313.4 jit_solution(16947448795203204090)
XLA Ops:
  0.7 0.7 select_reduce_fusion.2
  1.4 0.7 select_reduce_fusion.1
  2.2 0.1 reduce_sum.31
  2.4 0.9 select_reduce_fusion
  3.3 0.1 convert_convert_fusion
  3.4 2.3 broadcast_multiply_fusion.1.amp_ref
  5.7 141.9 %ladder.1 = bf16[8,2,256,256]{3,2,1,0:T(8,128)(2,1)} custom-call(bf16[32,16384]{1,0:T(8,128)(2,1)} %broadcast_multiply_fusion.1.amp_ref, bf16[2048,16384]{1,0:T(8,128)(2,1)} %w_ref.1), custom_call_target="tpu_custom_call" | custom-call | flops 34359738368 | bytes 67108864 | tf_op jit(solution)/shard_map/ladder/pallas_call | solution.py:315
  147.6 3.0 copy.14
  150.6 0.7 copy.11
  151.3 1.5 broadcast_multiply_fusion
  152.8 3.2 %reshape.231 = bf16[2,8,32,32,64]{4,3,2,1,0:T(8,128)(2,1)} reshape(bf16[2,2,2,2,32,8,256]{6,5,4,3,2,1,0:T(8,128)(2,1)S(1)} %bitcast.17) | data formatting | bytes 4194304 | tf_op jit(solution)/shard_map/reshape | solution.py:347
  155.9 1.7 fusion
  157.7 0.9 copy.10
  158.6 2.3 reshape.232.u_ref
  160.8 145.2 %cycle.1 = bf16[8,8,64,1024]{3,2,1,0:T(8,128)(2,1)} custom-call(bf16[2,8,32,1024]{3,2,1,0:T(8,128)(2,1)} %reshape.232.u_ref, bf16[16,8,64,1024]{3,2,1,0:T(8,128)(2,1)} %bitcast.20), custom_call_target="tpu_custom_call" | custom-call | flops 17179869184 | bytes 33554432 | tf_op jit(solution)/shard_map/cycle/pallas_call | solution.py:363
  306.0 7.3 %bitcast_multiply_fusion = bf16[4096,1024]{1,0:T(8,128)(2,1)} fusion(bf16[8,8,64,1024]{3,2,1,0:T(8,128)(2,1)} %cycle.1, bf16[1024]{0:T(1024)(128)(2,1)S(1)} %convert_convert_fusion.3), kind=kLoop, calls=%fused_computation | loop fusion | flops 4194304 | bytes 16779264 | tf_op jit(solution)/shard_map/mul | solution.py:395
  (6 shorter events, 0.2 us)

commit v2 on v1

--- a/solution.py
+++ b/solution.py
@@ -20,15 +20,6 @@
     return jnp.sum(
         jnp.where(irrep_of[:, None] == irrep_ids[None, :], virt_count[None, :], 0), axis=1
     )
-
-
-def pair_mask(virt_count, first_pos, length, slot_width):
-    position = first_pos + jnp.arange(length, dtype=jnp.int32)
-    irrep_of = position // (slot_width * slot_width)
-    slot_one = position // slot_width % slot_width
-    slot_two = position % slot_width
-    irrep_size = irrep_sizes(virt_count, irrep_of)
-    return ((slot_one < irrep_size) & (slot_two < irrep_size)).astype(jnp.float32)
 
 
 def slot_mask(virt_count, first_pos, length, slot_width):
@@ -101,10 +92,11 @@
     parts = range(len(PARTS))
     lag = 2
     for tick in range(chunks + lag * bits):
-        for step in range(bits, -1, -1):
-            chunk = tick - lag * step
-            if not 0 <= chunk < chunks:
-                continue
+        due = [(tick - lag * step, step) for step in range(bits, -1, -1)]
+        due = [(c, step) for c, step in due if 0 < c < chunks or (c, step) == (0, bits)]
+        if tick < bits:
+            due.insert(0, (0, tick))
+        for chunk, step in due:
             if step == 0:
                 own_ready(chunk)
             else:
@@ -122,7 +114,15 @@
                 copy_of(chunk, part, step).wait_send()
 
 
-def ladder_kernel(bits, amp_ref, w_ref, out_ref, held, w_buf, acc, away, near,
+def live_columns(count_ref, first, width):
+    block = VH * VH
+    live = count_ref[first // block]
+    slot_one = lax.rem(first, block) // VH + lax.broadcasted_iota(jnp.int32, (1, width), 1) // VH
+    slot_two = lax.broadcasted_iota(jnp.int32, (1, width), 1) % VH
+    return jnp.where((slot_one < live) & (slot_two < live), 1.0, 0.0)
+
+
+def ladder_kernel(bits, amp_ref, w_ref, count_ref, out_ref, held, w_buf, acc, away, near,
                   own_sem, w_sem, send_sem, recv_sem, sum_send, sum_recv, fin_send, fin_recv):
     me = lax.axis_index("virt")
     pair = lax.axis_index("pair")
@@ -161,8 +161,11 @@
             device_id_type=MESH,
         )
 
+    def at_tile(n):
+        return pl.ds(pl.multiple_of(n * tile, tile), tile)
+
     def fin_copy(n):
-        region = out_ref.at[n, pair]
+        region = out_ref.at[:, pair, :, :, at_tile(n)]
         return pltpu.make_async_remote_copy(
             src_ref=region, dst_ref=region, send_sem=fin_send.at[n],
             recv_sem=fin_recv.at[n], device_id={"virt": me, "pair": 1 - pair},
@@ -174,9 +177,8 @@
 
         @pl.loop(0, tiles)
         def _(n):
-            at = pl.ds(pl.multiple_of(n * tile, tile), tile)
             part = lax.dot_general(
-                merge_rows(held[c]), w_buf[c % slots, at, :], (((1,), (1,)), ((), ())),
+                merge_rows(held[c]), w_buf[c % slots, at_tile(n), :], (((1,), (1,)), ((), ())),
                 preferred_element_type=jnp.float32,
             )
             acc[n] = part if c == 0 else acc[n] + part
@@ -187,18 +189,37 @@
         if c + slots < chunks:
             w_copy(c + slots).start()
 
-    gather_waves(chunks, bits, copy_of, lambda c: own_copy(c).wait(), use)
+    def own_ready(c):
+        own_copy(c).wait()
+        keep = live_columns(count_ref, pair * (chunks * CHUNK) + c * CHUNK, CHUNK)
+        held[c, y, x, r] = held[c, y, x, r] * keep.astype(held.dtype)
+
+    gather_waves(chunks, bits, copy_of, own_ready, use)
+    fours = held.shape[3]
+    p_rows = held.shape[4]
 
     @pl.loop(0, tiles)
     def _(n):
         sum_copy(n).wait()
         total = acc[n, pl.ds(pl.multiple_of(pair * half, half), half), :] + near[n]
-        out_ref[n, pair] = total.astype(out_ref.dtype)
+        total = total * live_columns(count_ref, me * (tiles * tile) + n * tile, tile)
+        total = total.astype(out_ref.dtype)
+        for ox in range(2):
+            for o in range(fours):
+                first = (ox * fours + o) * p_rows
+                out_ref[bit_reverse(o, bits - 2), pair, ox, :, at_tile(n)] = total[
+                    first : first + p_rows
+                ]
         fin_copy(n).start()
 
     @pl.loop(0, tiles)
     def _(n):
         fin_copy(n).wait()
+
+
+def cycle_groups(all_i):
+    firsts = list(range(0, all_i - 2, 2))
+    return [(f, 2) for f in firsts] + [(all_i - 2, 1), (all_i - 1, 1)]
 
 
 def cycle_kernel(bits, u_ref, m_ref, out_ref, held, m_buf, away, near, own,
@@ -206,9 +227,9 @@
     me = lax.axis_index("virt")
     pair = lax.axis_index("pair")
     chunks = held.shape[1]
-    groups, irreps, rows, cols = away.shape
-    per_group = chunks // groups
-    a_count = held.shape[5]
+    all_i, irreps, slot_rows, cols = away.shape
+    split = chunks // all_i
+    groups = cycle_groups(all_i)
     per_irrep = (1 << bits) // irreps
     tile = min(256, cols)
     y, x, r = place_of(me, bits)
@@ -231,32 +252,38 @@
         m_copy(h).start()
     barrier(bits, me, pair)
 
+    def rows_of(ref, g, h):
+        return ref.at[pl.ds(groups[g][0], groups[g][1]), h]
+
     def sum_copy(g, h):
         return pltpu.make_async_remote_copy(
-            src_ref=away.at[g, h], dst_ref=near.at[g, h], send_sem=sum_send.at[g, h],
+            src_ref=rows_of(away, g, h), dst_ref=rows_of(near, g, h), send_sem=sum_send.at[g, h],
             recv_sem=sum_recv.at[g, h], device_id={"virt": me, "pair": 1 - pair},
             device_id_type=MESH,
         )
 
-    def out_copy(g, h, j):
-        size = rows // per_group
+    def out_copy(g, h):
         return pltpu.make_async_copy(
-            near.at[g, h, pl.ds(j * size, size), :],
-            out_ref.at[g * per_group + j, h], out_sem.at[g, h, j],
+            rows_of(near, g, h), rows_of(out_ref, g, h), out_sem.at[g, h]
         )
 
     def finish(g):
+        first, size = groups[g]
+
         @pl.loop(0, irreps)
         def _(h):
             sum_copy(g, h).wait_recv()
-            near[g, h] = (own[h] + near[g, h].astype(jnp.float32)).astype(near.dtype)
-            for j in range(per_group):
-                out_copy(g, h, j).start()
+            for j in range(size):
+                total = own[h, j] + near[first + j, h].astype(jnp.float32)
+                near[first + j, h] = total.astype(near.dtype)
+            out_copy(g, h).start()
 
     def use(c):
-        if (c + 1) % per_group:
+        ends = [(first + size) * split - 1 for first, size in groups]
+        if c not in ends:
             return
-        g = c // per_group
+        g = ends.index(c)
+        first, size = groups[g]
         if g:
             finish(g - 1)
 
@@ -266,28 +293,30 @@
                 m_copy(h).wait()
             pieces = []
             for side in (1 - pair, pair):
-                for j in range(per_group):
+                for i in range(first, first + size):
                     for s in range(per_irrep):
                         py, px, pr = place_of(h * per_irrep + s, bits)
-                        pieces.append(held[side, g * per_group + j, py, px, pr])
+                        for k in range(split):
+                            pieces.append(held[side, i * split + k, py, px, pr])
             left = merge_rows(jnp.stack(pieces))
             for n in range(cols // tile):
                 at = pl.ds(n * tile, tile)
                 part = jnp.dot(
                     left, merge_rows(m_buf[h, :, :, at]), preferred_element_type=jnp.float32
                 )
-                away[g, h, :, at] = part[:rows].astype(away.dtype)
-                own[h, :, at] = part[rows:]
+                for j in range(size):
+                    lo, hi = j * slot_rows, (size + j) * slot_rows
+                    away[first + j, h, :, at] = part[lo : lo + slot_rows].astype(away.dtype)
+                    own[h, j, :, at] = part[hi : hi + slot_rows]
             sum_copy(g, h).start()
 
     gather_waves(chunks, bits, copy_of, lambda c: own_copy(c).wait(), use)
-    finish(groups - 1)
-    for g in range(groups):
+    finish(len(groups) - 1)
+    for g in range(len(groups)):
         @pl.loop(0, irreps)
         def _(h):
             sum_copy(g, h).wait_send()
-            for j in range(per_group):
-                out_copy(g, h, j).wait()
+            out_copy(g, h).wait()
 
 
 def body(amplitudes, integrals, cycle_integrals, virt_count):
@@ -305,17 +334,16 @@
     dma = pltpu.SemaphoreType.DMA
     any_spec = pl.BlockSpec(memory_space=pl.ANY)
     parts = len(PARTS)
-    masked = amplitudes * pair_mask(virt_count, pair * cd_count, cd_count, slot_width)[
-        None, :
-    ].astype(jnp.bfloat16)
     chunks = cd_count // CHUNK
     tile = min(256, ab_count)
     tiles = ab_count // tile
     half = p_all // 2
     raw = pl.pallas_call(
         functools.partial(ladder_kernel, bits),
-        out_shape=jax.ShapeDtypeStruct((tiles, 2, half, tile), jnp.bfloat16),
-        in_specs=[any_spec, any_spec],
+        out_shape=jax.ShapeDtypeStruct(
+            (virt_devs // 4, 2, 2, p_rows, ab_count), jnp.bfloat16
+        ),
+        in_specs=[any_spec, any_spec, pl.BlockSpec(memory_space=pltpu.SMEM)],
         out_specs=pl.BlockSpec(memory_space=pltpu.VMEM),
         scratch_shapes=[
             pltpu.VMEM((chunks, 2, 2, virt_devs // 4, p_rows, CHUNK), jnp.bfloat16),
@@ -341,12 +369,8 @@
             transcendentals=0,
         ),
         name="ladder",
-    )(masked, integrals)
-    grid = raw.reshape((tiles,) + (2,) * bits + (p_rows, tile))
-    order = tuple(range(bits, 2, -1)) + (1, 2, bits + 1, 0, bits + 2)
-    rows = jnp.transpose(grid, order).reshape(p_all, ab_count)
-    keep_pairs = pair_mask(virt_count, virt * ab_count, ab_count, slot_width)[None, :]
-    ladder = rows * keep_pairs.astype(jnp.bfloat16)
+    )(amplitudes, integrals, virt_count)
+    ladder = raw.reshape(p_all, ab_count)
 
     a_count = ab_count // slot_width
     k_local = OJ // pair_devs
@@ -354,11 +378,12 @@
     own_k = lax.dynamic_slice_in_dim(
         ladder.reshape(2, half_i, OJ, a_count, slot_width), pair * k_local, k_local, 2
     )
+    split = 2 if a_count % 32 == 0 else 1
+    chunks = half_i * split
     sent = jnp.transpose(own_k, (0, 1, 3, 2, 4)).reshape(
-        2, half_i, a_count, k_local * slot_width
-    )
-    groups = half_i // 2
-    out_rows = half_i // groups * slot_width
+        2, chunks, a_count // split, k_local * slot_width
+    )
+    groups = len(cycle_groups(half_i))
     depth = k_local * slot_width
     cycle = pl.pallas_call(
         functools.partial(cycle_kernel, bits),
@@ -368,16 +393,18 @@
         in_specs=[any_spec, any_spec],
         out_specs=any_spec,
         scratch_shapes=[
-            pltpu.VMEM((2, half_i, 2, 2, virt_devs // 4, a_count, depth), jnp.bfloat16),
+            pltpu.VMEM(
+                (2, chunks, 2, 2, virt_devs // 4, a_count // split, depth), jnp.bfloat16
+            ),
             pltpu.VMEM((irrep_total, k_local, slot_width, jb_count), jnp.bfloat16),
-            pltpu.VMEM((groups, irrep_total, out_rows, jb_count), jnp.bfloat16),
-            pltpu.VMEM((groups, irrep_total, out_rows, jb_count), jnp.bfloat16),
-            pltpu.VMEM((irrep_total, out_rows, jb_count), jnp.float32),
-            dma((half_i,)),
+            pltpu.VMEM((half_i, irrep_total, slot_width, jb_count), jnp.bfloat16),
+            pltpu.VMEM((half_i, irrep_total, slot_width, jb_count), jnp.bfloat16),
+            pltpu.VMEM((irrep_total, 2, slot_width, jb_count), jnp.float32),
+            dma((chunks,)),
             dma((irrep_total,)),
-            dma((groups, irrep_total, 2)),
-            dma((half_i, parts, bits)),
-            dma((half_i, parts, bits)),
+            dma((groups, irrep_total)),
+            dma((chunks, parts, bits)),
+            dma((chunks, parts, bits)),
             dma((groups, irrep_total)),
             dma((groups, irrep_total)),
         ],

time: 314 us -> 311 us (level)
  other arithmetic: 15.5 us -> 8.25 us
  local copies, waits for them, and re-layouts: 10.1 us -> 13.7 us
    another operation x0 -> x1, local copies, waits for them, and re-layouts: none -> 7.07 us  [body(): ladder.reshape(2, half_i, OJ, a_count, slot_width)]
    reshape x2 -> x0, local copies, waits for them, and re-layouts: 6.18 us -> none  [the longest x1 3.17 us: body(): rows = jnp.transpose(grid, order).reshape(p_all, ab_count)]
    pallas_call x1, Pallas kernels: 142 us -> 146 us  [body(): pl.pallas_call(functools.partial(ladder_kernel, bits), out_shape=jax.Shap...]
    mul x2 -> x0, other arithmetic: 3.78 us -> none  [the longest x1 2.32 us: body(): amplitudes * pair_mask(virt_count, pair * cd_count, cd_count, slot_width)...]
where the time goes in v2:
time: 311 us
  Pallas kernels  289 us (93%)
  local copies, waits for them, and re-layouts  13.7 us (4%)
  other arithmetic  8.25 us (3%)
    pallas_call x1, Pallas kernels, body(): pl.pallas_call(functools.partial(ladder_kernel, bits), out_shape=jax.Shap...  146 us
    pallas_call x1, Pallas kernels, body(): pl.pallas_call(functools.partial(cycle_kernel, bits), out_shape=jax.Shape...  142 us
    mul x1, other arithmetic, body(): cycle.reshape(half_i * irrep_total * slot_width, jb_count)  7.47 us
    another operation x1, local copies, waits for them, and re-layouts, body(): ladder.reshape(2, half_i, OJ, a_count, slot_width)  7.07 us

profile of v2, /device:TPU:1, one launch (start us, length us, event | category | flops | bytes accessed | tf_op | source)
XLA Modules:
  0.0 311.2 jit_solution(9675978586525225797)
XLA Ops:
  0.7 0.7 select_reduce_fusion
  1.4 146.5 %ladder.1 = bf16[4,2,2,32,2048]{4,3,2,1,0:T(8,128)(2,1)} custom-call(bf16[32,16384]{1,0:T(8,128)(2,1)} %amp_ref.1, bf16[2048,16384]{1,0:T(8,128)(2,1)} %w_ref.1, s32[8]{0:T(128)} %count_ref.1), custom_call_target="tpu_custom_call" | custom-call | flops 34359738368 | bytes 67108864 | tf_op jit(solution)/shard_map/ladder/pallas_call | solution.py:341
  147.9 7.1 %reshape_reshape.3 = bf16[2,8,32,32,64]{4,3,2,1,0:T(8,128)(2,1)} reshape(bf16[4,2,2,32,2048]{4,3,2,1,0:T(8,128)(2,1)} %ladder.1) | data formatting | bytes 4194304 | tf_op jit(solution)/shard_map/reshape;reshape | solution.py:379
  155.0 2.1 constant_dynamic-slice_fusion
  157.1 0.9 copy.10
  158.0 2.3 reshape.80.u_ref
  160.3 142.1 %cycle.1 = bf16[8,8,64,1024]{3,2,1,0:T(8,128)(2,1)} custom-call(bf16[2,16,16,1024]{3,2,1,0:T(8,128)(2,1)} %reshape.80.u_ref, bf16[16,8,64,1024]{3,2,1,0:T(8,128)(2,1)} %bitcast.13), custom_call_target="tpu_custom_call" | custom-call | flops 17179869184 | bytes 33554432 | tf_op jit(solution)/shard_map/cycle/pallas_call | solution.py:388
  302.4 0.0 copy-start
  302.4 7.5 %bitcast_multiply_fusion = bf16[4096,1024]{1,0:T(8,128)(2,1)} fusion(bf16[8,8,64,1024]{3,2,1,0:T(8,128)(2,1)} %cycle.1, bf16[1024]{0:T(1024)(128)(2,1)S(1)} %convert_convert_fusion), kind=kLoop, calls=%fused_computation | loop fusion | flops 4194304 | bytes 16779264 | tf_op jit(solution)/shard_map/mul | solution.py:422
  309.9 0.0 copy-done
  309.9 1.3 copy.12
  (2 shorter events, 0.0 us)
Async XLA Ops:
  302.4 7.5 %copy-start = (bf16[4,2,2,32,2048]{4,3,2,1,0:T(8,128)(2,1)S(1)}, bf16[4,2,2,32,2048]{4,3,2,1,0:T(8,128)(2,1)}, u32[]{:S(2)}) copy-start(bf16[4,2,2,32,2048]{4,3,2,1,0:T(8,128)(2,1)} %ladder.1) | copy-start | bytes 6291460

commit v3 on v2

--- a/solution.py
+++ b/solution.py
@@ -12,7 +12,7 @@
 OJ = 32
 MESH = pl.DeviceIdType.MESH
 CHUNK = 1024
-PARTS = ((0, 384), (384, 384), (768, 256))
+WIDTHS = ((384, 384, 256), (512, 384, 128), (384, 384, 256), (384, 512, 128))
 
 
 def irrep_sizes(virt_count, irrep_of):
@@ -73,7 +73,8 @@
     done = order[:step]
     y, x, r = place_of(me, bits)
     high = len([b for b in done if b > 1])
-    off, width = PARTS[part]
+    widths = WIDTHS[chunk % len(WIDTHS)]
+    off, width = sum(widths[:part]), widths[part]
     at_y = pl.ds(0, 2) if 1 in done else pl.ds(y, 1)
     at_x = pl.ds(0, 2) if 0 in done else pl.ds(x, 1)
     at_r = pl.ds((r >> high) << high, 1 << high)
@@ -89,7 +90,7 @@
 
 
 def gather_waves(chunks, bits, copy_of, own_ready, use):
-    parts = range(len(PARTS))
+    parts = range(len(WIDTHS[0]))
     lag = 2
     for tick in range(chunks + lag * bits):
         due = [(tick - lag * step, step) for step in range(bits, -1, -1)]
@@ -333,7 +334,7 @@
     virt = lax.axis_index("virt")
     dma = pltpu.SemaphoreType.DMA
     any_spec = pl.BlockSpec(memory_space=pl.ANY)
-    parts = len(PARTS)
+    parts = len(WIDTHS[0])
     chunks = cd_count // CHUNK
     tile = min(256, ab_count)
     tiles = ab_count // tile
@@ -376,7 +377,10 @@
     k_local = OJ // pair_devs
     half_i = OI // 2
     own_k = lax.dynamic_slice_in_dim(
-        ladder.reshape(2, half_i, OJ, a_count, slot_width), pair * k_local, k_local, 2
+        ladder.reshape(2, half_i, OJ, ab_count), pair * k_local, k_local, 2
+    )
+    own_k = lax.optimization_barrier(own_k).reshape(
+        2, half_i, k_local, a_count, slot_width
     )
     split = 2 if a_count % 32 == 0 else 1
     chunks = half_i * split

time: 311 us -> 321 us (1.032)
  Pallas kernels: 289 us -> 301 us
    pallas_call x1, Pallas kernels: 146 us -> 154 us  [body(): pl.pallas_call(functools.partial(ladder_kernel, bits), out_shape=jax.Shap...]
    another operation x1 -> x0, local copies, waits for them, and re-layouts: 7.07 us -> none  [body(): ladder.reshape(2, half_i, OJ, a_count, slot_width)]
    pallas_call x1, Pallas kernels: 142 us -> 147 us  [body(): pl.pallas_call(functools.partial(cycle_kernel, bits), out_shape=jax.Shape...]
where the time goes in v3:
time: 321 us
  Pallas kernels  301 us (94%)
  local copies, waits for them, and re-layouts  11.1 us (3%)
  other arithmetic  8.25 us (3%)
    pallas_call x1, Pallas kernels, body(): pl.pallas_call(functools.partial(ladder_kernel, bits), out_shape=jax.Shap...  154 us
    pallas_call x1, Pallas kernels, body(): pl.pallas_call(functools.partial(cycle_kernel, bits), out_shape=jax.Shape...  147 us
    mul x1, other arithmetic, body(): cycle.reshape(half_i * irrep_total * slot_width, jb_count)  7.47 us

profile of v3, /device:TPU:1, one launch (start us, length us, event | category | flops | bytes accessed | tf_op | source)
XLA Modules:
  0.0 320.6 jit_solution(7633972704501095932)
XLA Ops:
  0.7 0.7 select_reduce_fusion
  1.4 154.0 %ladder.1 = bf16[4,2,2,32,2048]{4,3,2,1,0:T(8,128)(2,1)} custom-call(bf16[32,16384]{1,0:T(8,128)(2,1)} %amp_ref.1, bf16[2048,16384]{1,0:T(8,128)(2,1)} %w_ref.1, s32[8]{0:T(128)} %count_ref.1), custom_call_target="tpu_custom_call" | custom-call | flops 34359738368 | bytes 67108864 | tf_op jit(solution)/shard_map/ladder/pallas_call | solution.py:342
  155.4 1.3 constant_dynamic-slice_fusion
  156.7 2.2 reshape.83
  158.9 2.2 copy.7
  161.1 4.1 %reshape.84.u_ref = bf16[2,16,16,1024]{3,2,1,0:T(8,128)(2,1)} reshape(bf16[2,8,32,16,64]{4,3,2,1,0:T(8,128)(2,1)} %copy.7) | data formatting | bytes 2097152 | tf_op jit(solution)/shard_map/reshape | solution.py:387
  165.2 146.6 %cycle.1 = bf16[8,8,64,1024]{3,2,1,0:T(8,128)(2,1)} custom-call(bf16[2,16,16,1024]{3,2,1,0:T(8,128)(2,1)} %reshape.84.u_ref, bf16[16,8,64,1024]{3,2,1,0:T(8,128)(2,1)} %bitcast.13), custom_call_target="tpu_custom_call" | custom-call | flops 17179869184 | bytes 33554432 | tf_op jit(solution)/shard_map/cycle/pallas_call | solution.py:392
  311.8 0.0 copy-start
  311.8 7.5 %bitcast_multiply_fusion = bf16[4096,1024]{1,0:T(8,128)(2,1)} fusion(bf16[8,8,64,1024]{3,2,1,0:T(8,128)(2,1)} %cycle.1, bf16[1024]{0:T(1024)(128)(2,1)S(1)} %convert_convert_fusion), kind=kLoop, calls=%fused_computation | loop fusion | flops 4194304 | bytes 16779264 | tf_op jit(solution)/shard_map/mul | solution.py:426
  319.3 0.0 copy-done
  319.3 1.3 copy.9
  (2 shorter events, 0.0 us)
Async XLA Ops:
  311.8 7.5 %copy-start = (bf16[4,2,2,32,2048]{4,3,2,1,0:T(8,128)(2,1)S(1)}, bf16[4,2,2,32,2048]{4,3,2,1,0:T(8,128)(2,1)}, u32[]{:S(2)}) copy-start(bf16[4,2,2,32,2048]{4,3,2,1,0:T(8,128)(2,1)} %ladder.1) | copy-start | bytes 6291460
